TPU v7x, 512 devices: a whole 4x4x16 slice. The times are simulated.
512 devices in a mesh: mem: 32 (over z_hi, y, x), tile: 16 (over z_lo, core).
Axes of the slice: x: 4, y: 4, z: 16 (z_hi: 2, z_lo: 8; z = z_hi * 8 + z_lo), core: 2. Of those that a mesh axis runs over, the one named last changes fastest.
Arguments:
- ensemble_state: bfloat16 [128, 32, 128, 768], P('mem', 'tile'), may hold values from -6 to 6
- obs_members: bfloat16 [128, 32, 128, 128], P('mem', 'tile'), may hold values from -38 to 38
- obs_values: float32 [32, 128, 128], P('tile', 'mem'), may hold values from -8 to 8
- obs_variance: float32 [32, 128, 128], P('tile', 'mem'), may hold values from 0.02 to 1
- obs_counts: int32 [32, 128], P('tile', 'mem'), may hold values from 0 to 128, as said below
Outputs:
- analysis: bfloat16 [128, 32, 128, 768], P('mem', 'tile')
Inputs may be any that keep to these rules, and one draw needn't show every extreme that they name: obs_counts[i, j] observations of block (i, j) fill its first slots of obs_members, obs_values and obs_variance; later slots carry no observation. Some block holds 128.
All inputs are finite; a program needn't handle non-finite values.
Results may differ from a plain program's by a relative error of at most 0.012.
The roundings to bfloat16 on the way count: a program that leaves them out, or rounds other values in their place, can miss the bound.
Values may be sent and summed in bfloat16 or wider, within the bound.
A program may use at most 64 MiB of HBM per device.

v0:
```python
import math

import jax
import jax.numpy as jnp
from jax import lax
from jax.sharding import PartitionSpec as P

NS_ITERS = 12


def with_halo(value, sides, width):
    for axis, dim in sides:
        size, length = (lax.axis_size(axis), value.shape[dim])
        up = [(i, (i + 1) % size) for i in range(size - 1)]
        down = [(j, i) for i, j in up]
        last = lax.slice_in_dim(value, length - width, length, axis=dim)
        initial = lax.slice_in_dim(value, 0, width, axis=dim)
        before = lax.ppermute(last, axis, up)
        after = lax.ppermute(initial, axis, down)
        value = jnp.concatenate([before, value, after], axis=dim)
    return value


def near_sum(padded, block_rows, block_cols):
    result = None
    for row_step in range(-2, 3):
        for col_step in range(-2, 3):
            weight = math.exp(-(row_step * row_step + col_step * col_step) / 4.0)
            shifted = padded[
                2 + row_step : 2 + row_step + block_rows, 2 + col_step : 2 + col_step + block_cols
            ]
            result = weight * shifted if result is None else result + weight * shifted
    return result


def inverse_root(system):
    count = system.shape[-1]
    scale_norm = jnp.sqrt(jnp.sum(system * system, axis=(-2, -1)))
    iterate = system / scale_norm[..., None, None]
    identity = jnp.eye(count, dtype=jnp.float32)
    inverse = jnp.broadcast_to(identity, system.shape)
    for sweep_index in range(NS_ITERS):
        factor = 1.5 * identity - 0.5 * jnp.matmul(
            inverse, iterate, precision=lax.Precision.HIGHEST
        )
        iterate = jnp.matmul(iterate, factor, precision=lax.Precision.HIGHEST)
        inverse = jnp.matmul(factor, inverse, precision=lax.Precision.HIGHEST)
    return inverse / jnp.sqrt(scale_norm)[..., None, None]


def block_terms(scaled, innovation):
    gram_blocks = jnp.einsum("ijkc,ijlc->ijkl", scaled, scaled, preferred_element_type=jnp.float32)
    drive_terms = jnp.einsum(
        "ijkc,ijc->ijk", scaled, innovation, preferred_element_type=jnp.float32
    )
    return (gram_blocks, drive_terms)


def on_device(ensemble_state, obs_members, obs_values, obs_variance, obs_counts):
    obs_panel, state_panel = (
        lax.all_to_all(obs_members, "mem", split_axis=2, concat_axis=0, tiled=True),
        lax.all_to_all(ensemble_state, "mem", split_axis=2, concat_axis=0, tiled=True),
    )
    member_count = obs_panel.shape[0]
    block_rows = obs_values.shape[0]
    block_cols = obs_values.shape[1]
    obs_mean = jnp.sum(obs_panel, axis=0, dtype=jnp.float32) / member_count
    slot_index = lax.broadcasted_iota(jnp.int32, obs_values.shape, 2)
    usable = slot_index < obs_counts[:, :, None]
    root_weight = jnp.where(usable, 1.0 / jnp.sqrt(obs_variance), jnp.float32(0.0))
    centred = jnp.transpose(obs_panel, (1, 2, 0, 3)).astype(jnp.float32) - obs_mean[:, :, None, :]
    scaled = (centred * root_weight[:, :, None, :]).astype(jnp.bfloat16)
    innovation = (root_weight * (obs_values - obs_mean)).astype(jnp.bfloat16)
    gram_blocks, drive_terms = block_terms(scaled, innovation)
    gram_wide, drive_wide = (
        with_halo(gram_blocks, (("mem", 1), ("tile", 0)), 2),
        with_halo(drive_terms, (("mem", 1), ("tile", 0)), 2),
    )
    total_gram = near_sum(gram_wide, block_rows, block_cols)
    total_drive = near_sum(drive_wide, block_rows, block_cols)
    system = total_gram + (member_count - 1) * jnp.eye(member_count, dtype=jnp.float32)
    inverse = inverse_root(system)
    inner = jnp.einsum("ijkl,ijl->ijk", inverse, total_drive, precision=lax.Precision.HIGHEST)
    mean_weight = jnp.einsum("ijkl,ijl->ijk", inverse, inner, precision=lax.Precision.HIGHEST)
    mixing = (math.sqrt(member_count - 1) * inverse + mean_weight[..., :, None]).astype(
        jnp.bfloat16
    )
    state_mean = jnp.sum(state_panel, axis=0, dtype=jnp.float32) / member_count
    anomaly = (state_panel.astype(jnp.float32) - state_mean).astype(jnp.bfloat16)
    update = jnp.einsum("kijf,ijkl->lijf", anomaly, mixing, preferred_element_type=jnp.float32)
    analysis = (state_mean + update).astype(jnp.bfloat16)
    return lax.all_to_all(analysis, "mem", split_axis=0, concat_axis=2, tiled=True)


def solution(mesh):
    placed = (
        P("mem", "tile", None, None),
        P("mem", "tile", None, None),
        P("tile", "mem", None),
        P("tile", "mem", None),
        P("tile", "mem"),
    )
    return jax.shard_map(
        on_device,
        mesh=mesh,
        in_specs=placed,
        out_specs=P("mem", "tile", None, None),
        check_vma=False,
    )
```

profile of v0, /device:TPU:32, one launch (start us, length us, event | category | flops | bytes accessed | tf_op | source)
XLA Modules:
  0.0 302.5 jit_solution(514366359302999721)
XLA Ops:
  0.0 1.9 copy.45
  1.9 19.7 %all-to-all-start.1 = ((bf16[4,2,128,128]{3,0,1,2:T(4,128)(2,1)}), bf16[4,2,128,128]{3,0,1,2:T(4,128)(2,1)S(1)}, u32[]{:S(2)}, u32[]{:S(2)}) async-start(bf16[4,2,128,128]{3,0,1,2:T(4,128)(2,1)} %copy.45), calls=%async_computation.1 | async-start | bytes 524288 | tf_op jit(solution)/shard_map/all_to_all | solution.py:61
  22.3 25.4 %all-to-all-done.1 = bf16[4,2,128,128]{3,0,1,2:T(4,128)(2,1)S(1)} async-done(((bf16[4,2,128,128]{3,0,1,2:T(4,128)(2,1)}), bf16[4,2,128,128]{3,0,1,2:T(4,128)(2,1)S(1)}, u32[]{:S(2)}, u32[]{:S(2)}) %all-to-all-start.1) | async-done | bytes 262176 | tf_op jit(solution)/shard_map/all_to_all | solution.py:61
  50.2 2.2 collective-permute-start
  52.4 1.3 collective-permute-start.1
  53.7 3.8 %copy.42 = bf16[4,2,128,768]{3,0,1,2:T(4,128)(2,1)} copy(bf16[4,2,128,768]{3,2,1,0:T(8,128)(2,1)} %param.5) | data formatting | bytes 3145728 | tf_op args[0]
  57.5 17.5 %all-to-all-start = ((bf16[4,2,128,768]{3,0,1,2:T(4,128)(2,1)}), bf16[4,2,128,768]{3,0,1,2:T(4,128)(2,1)S(1)}, u32[]{:S(2)}, u32[]{:S(2)}) async-start(bf16[4,2,128,768]{3,0,1,2:T(4,128)(2,1)} %copy.42), calls=%async_computation | async-start | bytes 3145728 | tf_op jit(solution)/shard_map/all_to_all | solution.py:62
  75.1 1.9 collective-permute-start.2
  77.0 3.6 %collective-permute-start.3 = (f32[2,8,128,128]{3,2,1,0:T(8,128)S(1)}, f32[2,8,128,128]{3,2,1,0:T(8,128)S(1)}, u32[]{:S(2)}, u32[]{:S(2)}) collective-permute-start(f32[2,8,128,128]{3,2,1,0:T(8,128)S(1)} %pad_maximum_fusion.1), channel_id=1, source_target_pairs={{1,0},{2,1},{3,2},{4,3},{5,4},{6,5},{7,6},{8,7},{9,8},{10,9},{11,1... | collective-permute-start | bytes 3145736 | tf_op jit(solution)/shard_map/ppermute | solution.py:19
  80.9 3.7 %collective-permute-start.4 = (f32[2,2,128]{2,1,0:T(2,128)S(1)}, f32[2,2,128]{2,1,0:T(2,128)S(1)}, u32[]{:S(2)}, u32[]{:S(2)}) collective-permute-start(f32[2,2,128]{2,1,0:T(2,128)S(1)} %get-tuple-element.15), channel_id=1, source_target_pairs={{0,16},{16,32},{32,48},{48,64},{64,80},{80,96},{96,112},{112,128},... | collective-permute-start | bytes 6152 | tf_op jit(solution)/shard_map/ppermute | solution.py:18
  84.6 1.3 collective-permute-start.5
  86.0 4.2 %collective-permute-done.5 = f32[2,2,128]{2,1,0:T(2,128)S(1)} collective-permute-done((f32[2,2,128]{2,1,0:T(2,128)S(1)}, f32[2,2,128]{2,1,0:T(2,128)S(1)}, u32[]{:S(2)}, u32[]{:S(2)}) %collective-permute-start.5) | collective-permute-done | bytes 2080 | tf_op jit(solution)/shard_map/ppermute | solution.py:19
  90.1 1.9 collective-permute-start.6
  92.0 3.6 %collective-permute-start.7 = (f32[2,8,128]{2,1,0:T(8,128)S(1)}, f32[2,8,128]{2,1,0:T(8,128)S(1)}, u32[]{:S(2)}, u32[]{:S(2)}) collective-permute-start(f32[2,8,128]{2,1,0:T(8,128)S(1)} %pad_maximum_fusion.5), channel_id=1, source_target_pairs={{1,0},{2,1},{3,2},{4,3},{5,4},{6,5},{7,6},{8,7},{9,8},{10,9},{11,1... | collective-permute-start | bytes 24584 | tf_op jit(solution)/shard_map/ppermute | solution.py:19
  95.7 64.5 %collective-permute-done.6 = f32[2,8,128]{2,1,0:T(8,128)S(1)} collective-permute-done((f32[2,8,128]{2,1,0:T(8,128)S(1)}, f32[2,8,128]{2,1,0:T(8,128)S(1)}, u32[]{:S(2)}, u32[]{:S(2)}) %collective-permute-start.6) | collective-permute-done | bytes 8224 | tf_op jit(solution)/shard_map/ppermute | solution.py:18
  160.9 1.7 multiply_reduce_fusion
  186.7 1.1 fusion.117
  188.3 2.2 copy.53
  190.5 5.0 %reshape.41 = f32[128,2,4,768]{3,0,2,1:T(8,128)} reshape(f32[32,4,2,4,768]{4,1,0,3,2:T(4,128)} %copy.53) | data formatting | bytes 6291456 | tf_op jit(solution)/shard_map/convert_element_type | solution.py:88
  195.4 2.6 convert_reduce_fusion
  198.3 2.7 fusion.1
  201.0 1.2 copy.55
  202.2 98.1 %all_to_all.36 = bf16[128,2,4,768]{3,2,1,0:T(4,128)(2,1)S(1)} all-to-all(bf16[128,2,4,768]{3,2,1,0:T(4,128)(2,1)S(1)} %copy.55), channel_id=1, replica_groups=mesh['mem'=32,'tile'=16] {'mem'}, dimensions={0} | all-to-all | bytes 3145728 | tf_op jit(solution)/shard_map/all_to_all | solution.py:92
  300.9 1.3 all_to_all.32
  (68 shorter events, 29.2 us)
Async XLA Ops:
  1.9 45.9 %all-to-all-start.1 = ((bf16[4,2,128,128]{3,0,1,2:T(4,128)(2,1)}), bf16[4,2,128,128]{3,0,1,2:T(4,128)(2,1)S(1)}, u32[]{:S(2)}, u32[]{:S(2)}) async-start(bf16[4,2,128,128]{3,0,1,2:T(4,128)(2,1)} %copy.45), calls=%async_computation.1 | async-start | bytes 524288 | tf_op jit(solution)/shard_map/all_to_all | solution.py:61
  50.2 24.8 %collective-permute-start = (f32[2,2,128,128]{3,2,1,0:T(8,128)}, f32[2,2,128,128]{3,2,1,0:T(8,128)S(1)}, u32[]{:S(2)}, u32[]{:S(2)}) collective-permute-start(f32[2,2,128,128]{3,2,1,0:T(8,128)} %get-tuple-element.11), channel_id=1, source_target_pairs={{0,16},{16,32},{32,48},{48,64},{64,80},{80,96},{96,112},{112,128},... | collective-permute-start | bytes 786440 | tf_op jit(solution)/shard_map/ppermute | solution.py:18
  52.4 22.6 %collective-permute-start.1 = (f32[2,2,128,128]{3,2,1,0:T(8,128)S(1)}, f32[2,2,128,128]{3,2,1,0:T(8,128)S(1)}, u32[]{:S(2)}, u32[]{:S(2)}) collective-permute-start(f32[2,2,128,128]{3,2,1,0:T(8,128)S(1)} %get-tuple-element.12), channel_id=1, source_target_pairs={{16,0},{32,16},{48,32},{64,48},{80,64},{96,80},{112,96},{128,112},... | collective-permute-start | bytes 786440 | tf_op jit(solution)/shard_map/ppermute | solution.py:19
  57.5 130.3 %all-to-all-start = ((bf16[4,2,128,768]{3,0,1,2:T(4,128)(2,1)}), bf16[4,2,128,768]{3,0,1,2:T(4,128)(2,1)S(1)}, u32[]{:S(2)}, u32[]{:S(2)}) async-start(bf16[4,2,128,768]{3,0,1,2:T(4,128)(2,1)} %copy.42), calls=%async_computation | async-start | bytes 3145728 | tf_op jit(solution)/shard_map/all_to_all | solution.py:62
  75.1 85.2 %collective-permute-start.2 = (f32[2,8,128,128]{3,2,1,0:T(8,128)S(1)}, f32[2,8,128,128]{3,2,1,0:T(8,128)S(1)}, u32[]{:S(2)}, u32[]{:S(2)}) collective-permute-start(f32[2,8,128,128]{3,2,1,0:T(8,128)S(1)} %pad_maximum_fusion.1), channel_id=1, source_target_pairs={{0,1},{1,2},{2,3},{3,4},{4,5},{5,6},{6,7},{7,8},{8,9},{9,10},{10,1... | collective-permute-start | bytes 3145736 | tf_op jit(solution)/shard_map/ppermute | solution.py:18
  77.0 83.2 %collective-permute-start.3 = (f32[2,8,128,128]{3,2,1,0:T(8,128)S(1)}, f32[2,8,128,128]{3,2,1,0:T(8,128)S(1)}, u32[]{:S(2)}, u32[]{:S(2)}) collective-permute-start(f32[2,8,128,128]{3,2,1,0:T(8,128)S(1)} %pad_maximum_fusion.1), channel_id=1, source_target_pairs={{1,0},{2,1},{3,2},{4,3},{5,4},{6,5},{7,6},{8,7},{9,8},{10,9},{11,1... | collective-permute-start | bytes 3145736 | tf_op jit(solution)/shard_map/ppermute | solution.py:19
  80.9 5.0 %collective-permute-start.4 = (f32[2,2,128]{2,1,0:T(2,128)S(1)}, f32[2,2,128]{2,1,0:T(2,128)S(1)}, u32[]{:S(2)}, u32[]{:S(2)}) collective-permute-start(f32[2,2,128]{2,1,0:T(2,128)S(1)} %get-tuple-element.15), channel_id=1, source_target_pairs={{0,16},{16,32},{32,48},{48,64},{64,80},{80,96},{96,112},{112,128},... | collective-permute-start | bytes 6152 | tf_op jit(solution)/shard_map/ppermute | solution.py:18
  84.6 5.5 %collective-permute-start.5 = (f32[2,2,128]{2,1,0:T(2,128)S(1)}, f32[2,2,128]{2,1,0:T(2,128)S(1)}, u32[]{:S(2)}, u32[]{:S(2)}) collective-permute-start(f32[2,2,128]{2,1,0:T(2,128)S(1)} %get-tuple-element.16), channel_id=1, source_target_pairs={{16,0},{32,16},{48,32},{64,48},{80,64},{96,80},{112,96},{128,112},... | collective-permute-start | bytes 6152 | tf_op jit(solution)/shard_map/ppermute | solution.py:19
  90.1 70.1 %collective-permute-start.6 = (f32[2,8,128]{2,1,0:T(8,128)S(1)}, f32[2,8,128]{2,1,0:T(8,128)S(1)}, u32[]{:S(2)}, u32[]{:S(2)}) collective-permute-start(f32[2,8,128]{2,1,0:T(8,128)S(1)} %pad_maximum_fusion.5), channel_id=1, source_target_pairs={{0,1},{1,2},{2,3},{3,4},{4,5},{5,6},{6,7},{7,8},{8,9},{9,10},{10,1... | collective-permute-start | bytes 24584 | tf_op jit(solution)/shard_map/ppermute | solution.py:18
  92.0 68.2 %collective-permute-start.7 = (f32[2,8,128]{2,1,0:T(8,128)S(1)}, f32[2,8,128]{2,1,0:T(8,128)S(1)}, u32[]{:S(2)}, u32[]{:S(2)}) collective-permute-start(f32[2,8,128]{2,1,0:T(8,128)S(1)} %pad_maximum_fusion.5), channel_id=1, source_target_pairs={{1,0},{2,1},{3,2},{4,3},{5,4},{6,5},{7,6},{8,7},{9,8},{10,9},{11,1... | collective-permute-start | bytes 24584 | tf_op jit(solution)/shard_map/ppermute | solution.py:19
where the time goes:
time: 307 us; the launch traced here: 302 us
  blocking collectives  98.1 us (32%)
  waiting for transfers between devices  94.1 us (31%)
  starting transfers between devices  56.8 us (19%)
  matrix products  28.2 us (9%)
  local copies, waits for them, and re-layouts  17.5 us (6%)
  other arithmetic  7.06 us (2%)
    all_to_all x1, blocking collectives, on_device(): lax.all_to_all(analysis, 'mem', split_axis=0, concat_axis=2, tiled=True)  98.1 us
    ppermute x4, waiting for transfers between devices, with_halo(): before = lax.ppermute(last, axis, up)  64.5 us
    all_to_all x1, waiting for transfers between devices, on_device(): lax.all_to_all(obs_members, 'mem', split_axis=2, concat_axis=0, tiled=True)  25.4 us
    all_to_all x1, starting transfers between devices, on_device(): lax.all_to_all(obs_members, 'mem', split_axis=2, concat_axis=0, tiled=True)  19.7 us
    all_to_all x1, starting transfers between devices, on_device(): lax.all_to_all(ensemble_state, 'mem', split_axis=2, concat_axis=0, tiled=...  17.5 us
    ppermute x4, starting transfers between devices, with_halo(): after = lax.ppermute(initial, axis, down)  9.87 us
    ppermute x4, starting transfers between devices, with_halo(): before = lax.ppermute(last, axis, up)  9.78 us
    dot_general x12, matrix products, inverse_root(): jnp.matmul(inverse, iterate, precision=lax.Precision.HIGHEST)  7.97 us
  transfers between devices with their start and end apart: 10, of which 3 were waited for; matrix products, arithmetic and copies ran while one was open for 11% of the time, Pallas kernels for 0%

commit v1 on v0

v1 whole, which is shorter than its diff:
```python
import functools
import math

import jax
import jax.numpy as jnp
from jax import lax
from jax.experimental import pallas as pl
from jax.experimental.pallas import tpu as pltpu
from jax.sharding import PartitionSpec as P

NS_ITERS = 12
MESH = pl.DeviceIdType.MESH
BF = jnp.bfloat16
F32 = jnp.float32
W1 = math.exp(-0.25)
W2 = math.exp(-1.0)
NEAR = (W2, W1, 1.0, W1, W2)
K = 128
EXT = 144
ROWS = 136


def iota(shape, dim):
    return lax.broadcasted_iota(jnp.int32, shape, dim)


def dot(a, b):
    return lax.dot_general(a, b, (((1,), (0,)), ((), ())), preferred_element_type=F32)


def dot_t(a, b):
    return lax.dot_general(a, b, (((1,), (1,)), ((), ())), preferred_element_type=F32)


def one_hot(hit):
    return jnp.where(hit, 1.0, 0.0).astype(BF)


def split2(value):
    high = value.astype(BF)
    return high, (value - high.astype(F32)).astype(BF)


def split3(value):
    high = value.astype(BF)
    rest = value - high.astype(F32)
    mid = rest.astype(BF)
    return high, mid, (rest - mid.astype(F32)).astype(BF)


def right2(high, low):
    pair = jnp.concatenate([high, low], axis=1)
    return jnp.concatenate([pair, pair], axis=0)


def mul2(left, right):
    both = dot(jnp.concatenate(split2(left), axis=1), right)
    return both[:, :K] + both[:, K:]


def right3(parts):
    high, mid, low = parts
    return right2(high, mid), jnp.concatenate([high, low], axis=0)


def mul3(left, right):
    high, mid, low = split3(left)
    both = dot(jnp.concatenate([high, mid], axis=1), right[0])
    small = dot(jnp.concatenate([low, high], axis=1), right[1])
    return both[:, :K] + (both[:, K:] + small)


def kernel(
    state, obs, values, variance, counts, out,
    obs_out, obs_in, state_out, state_in, res_out, res_in,
    scaled, grams, sums, above, below, root, inv, mix, perm, perm_back,
    obs_s, obs_r, state_s, state_r, col_s, col_r, row_s, row_r, res_s, res_r,
):
    mem, tile = lax.axis_index("mem"), lax.axis_index("tile")
    mems, tiles = 32, 16
    z, y, x = mem // 16, lax.rem(mem // 4, 4), lax.rem(mem, 4)

    def partner(step):
        pz = lax.rem(z + step // 16, 2)
        py = lax.rem(y + lax.rem(step // 4, 4), 4)
        px = lax.rem(x + lax.rem(step, 4), 4)
        return pz * 16 + py * 4 + px

    barrier = pltpu.get_barrier_semaphore()

    @pl.loop(1, mems)
    def _(step):
        pl.semaphore_signal(barrier, inc=1, device_id={"mem": partner(step)}, device_id_type=MESH)

    @pl.when(tile > 0)
    def _():
        pl.semaphore_signal(barrier, inc=1, device_id={"tile": tile - 1}, device_id_type=MESH)

    @pl.when(tile < tiles - 1)
    def _():
        pl.semaphore_signal(barrier, inc=1, device_id={"tile": tile + 1}, device_id_type=MESH)

    r, c = iota((64, 64), 0), iota((64, 64), 1)
    pack = one_hot(c == (r % 4) * 16 + (r // 16) * 4 + (r // 4) % 4)
    unpack = one_hot(r == (c % 4) * 16 + (c // 16) * 4 + (c // 4) % 4)

    def packed(source, target):
        for i in range(2):
            for q in range(8):
                rows = jnp.concatenate([source[k, i, 16 * q:16 * q + 16, :] for k in range(4)], axis=0)
                moved = dot(pack, rows).astype(BF)
                for d in range(4):
                    target[4 * q + d, i] = moved[16 * d:16 * d + 16]

    packed(obs, obs_out)
    obs_in[mem] = obs_out[mem]

    @pl.when(tile == 0)
    def _():
        pl.semaphore_wait(barrier, mems)

    @pl.when(tile == tiles - 1)
    def _():
        pl.semaphore_wait(barrier, mems)

    @pl.when(jnp.logical_and(tile > 0, tile < tiles - 1))
    def _():
        pl.semaphore_wait(barrier, mems + 1)

    def send_all(source, target, send, receive, first, last):
        @pl.loop(first, last)
        def _(step):
            to = partner(step)
            pltpu.make_async_remote_copy(
                src_ref=source.at[to], dst_ref=target.at[mem], send_sem=send, recv_sem=receive,
                device_id={"mem": to}, device_id_type=MESH,
            ).start()

    def take(ref, semaphore):
        pltpu.make_async_copy(ref, ref, semaphore).wait()

    send_all(obs_out, obs_in, obs_s, obs_r, 16, 32)
    send_all(obs_out, obs_in, obs_s, obs_r, 1, 16)

    packed(state, state_out)
    state_in[mem] = state_out[mem]
    r, c = iota((512, 512), 0), iota((512, 512), 1)
    perm[...] = one_hot(c == ((r // 4) % 32) * 16 + (r // 128) * 4 + r % 4)
    perm_back[...] = one_hot(r == ((c // 4) % 32) * 16 + (c // 128) * 4 + c % 4)

    some = pl.ds(0, mems - 1)
    take(obs_out.at[some], obs_s)
    send_all(state_out, state_in, state_s, state_r, 16, 32)
    take(obs_in.at[some], obs_r)

    slot = iota((1, 128), 1)
    for i in range(2):
        wide = dot(perm[...], obs_in[:, i].reshape(512, 128))
        for j in range(4):
            member = wide[128 * j:128 * j + 128]
            mean = jnp.sum(member, axis=0, keepdims=True) * (1.0 / K)
            weight = jnp.where(slot < counts[i, j], 1.0 / jnp.sqrt(variance[i, j:j + 1, :]), 0.0)
            innovation = weight * (values[i, j:j + 1, :] - mean)
            scaled[j + 2, i, 0:K] = ((member - mean) * weight).astype(BF)
            scaled[j + 2, i, K:EXT] = jnp.where(
                iota((16, 128), 0) == 0, jnp.broadcast_to(innovation, (16, 128)), 0.0
            ).astype(BF)

    def to_left():
        return pltpu.make_async_remote_copy(
            src_ref=scaled.at[pl.ds(2, 2)], dst_ref=scaled.at[pl.ds(6, 2)], send_sem=col_s.at[0],
            recv_sem=col_r.at[0], device_id={"mem": mem - 1}, device_id_type=MESH)

    def to_right():
        return pltpu.make_async_remote_copy(
            src_ref=scaled.at[pl.ds(4, 2)], dst_ref=scaled.at[pl.ds(0, 2)], send_sem=col_s.at[1],
            recv_sem=col_r.at[1], device_id={"mem": mem + 1}, device_id_type=MESH)

    @pl.when(mem > 0)
    def _():
        to_left().start()

    @pl.when(mem < mems - 1)
    def _():
        to_right().start()

    @pl.when(mem == 0)
    def _():
        scaled[0:2] = jnp.zeros((2, 2, EXT, 128), BF)

    @pl.when(mem == mems - 1)
    def _():
        scaled[6:8] = jnp.zeros((2, 2, EXT, 128), BF)

    def gram(col):
        for i in range(2):
            grams[col, i] = dot_t(scaled[col, i], scaled[col, i, 0:K])[:ROWS]

    for col in range(2, 6):
        gram(col)

    @pl.when(mem > 0)
    def _():
        to_left().wait_send()
        to_right().wait_recv()

    @pl.when(mem < mems - 1)
    def _():
        to_right().wait_send()
        to_left().wait_recv()

    for col in (0, 1, 6, 7):
        gram(col)
    for i in range(2):
        for j in range(4):
            total = NEAR[0] * grams[j, i]
            for b in range(1, 5):
                total = total + NEAR[b] * grams[j + b, i]
            sums[i, j] = total

    def to_above():
        return pltpu.make_async_remote_copy(
            src_ref=sums, dst_ref=below, send_sem=row_s.at[0], recv_sem=row_r.at[0],
            device_id={"tile": tile - 1}, device_id_type=MESH)

    def to_below():
        return pltpu.make_async_remote_copy(
            src_ref=sums, dst_ref=above, send_sem=row_s.at[1], recv_sem=row_r.at[1],
            device_id={"tile": tile + 1}, device_id_type=MESH)

    @pl.when(tile > 0)
    def _():
        to_above().start()

    @pl.when(tile < tiles - 1)
    def _():
        to_below().start()

    @pl.when(tile == 0)
    def _():
        above[...] = jnp.zeros(above.shape, F32)

    @pl.when(tile == tiles - 1)
    def _():
        below[...] = jnp.zeros(below.shape, F32)

    @pl.when(tile > 0)
    def _():
        to_above().wait_send()
        to_below().wait_recv()

    @pl.when(tile < tiles - 1)
    def _():
        to_below().wait_send()
        to_above().wait_recv()

    send_all(state_out, state_in, state_s, state_r, 1, 16)

    eye = jnp.where(iota((K, K), 0) == iota((K, K), 1), 1.0, 0.0).astype(F32)
    drives, norms = [], []
    for i in range(2):
        for j in range(4):
            b = 4 * i + j
            if i == 0:
                total = sums[0, j] + W1 * sums[1, j] + (W2 * above[0, j] + W1 * above[1, j]) + W2 * below[0, j]
            else:
                total = sums[1, j] + W1 * sums[0, j] + W2 * above[1, j] + (W1 * below[0, j] + W2 * below[1, j])
            system = total[:K] + (K - 1) * eye
            norm = jnp.sqrt(jnp.sum(jnp.sum(system * system, axis=1, keepdims=True), axis=0, keepdims=True))
            drives.append(total[K:ROWS])
            norms.append(norm)
            first = system / norm
            factor = 1.5 * eye - 0.5 * first
            right = right3(split3(factor))
            root[b] = mul3(mul3(first, right), right)
            inv[b] = factor

    for b in range(8):
        factor = 1.5 * eye - 0.5 * root[b]
        right = right3(split3(factor))
        inv[b] = mul3(inv[b], right)
        root[b] = mul3(mul3(root[b], right), right)

    @pl.loop(2, NS_ITERS - 1)
    def _(sweep):
        for b in range(8):
            factor = 1.5 * eye - 0.5 * root[b]
            right = right2(*split2(factor))
            inv[b] = mul2(inv[b], right)
            root[b] = mul2(mul2(root[b], right), right)

    for b in range(8):
        factor = 1.5 * eye - 0.5 * root[b]
        inverse = mul2(inv[b], right2(*split2(factor))) / jnp.sqrt(norms[b])
        right = right2(*split2(inverse))
        shift = mul2(mul2(drives[b], right), right)[0:1]
        mix[b] = (math.sqrt(K - 1) * inverse + shift).astype(BF)

    take(state_out.at[some], state_s)
    take(state_in.at[some], state_r)

    def send_result(i, first, last):
        send_all(res_out.at[i], res_in.at[i], res_s.at[i], res_r.at[i], first, last)

    for i in range(2):
        wide = dot(perm[...], state_in[:, i].reshape(512, 768))
        rows = []
        for j in range(4):
            member = wide[128 * j:128 * j + 128]
            mean = jnp.sum(member, axis=0, keepdims=True) * (1.0 / K)
            rows.append((mean + dot(mix[4 * i + j], (member - mean).astype(BF))).astype(BF))
        moved = dot(perm_back[...], jnp.concatenate(rows, axis=0)).astype(BF)
        res_out[i] = moved.reshape(32, 16, 768)
        send_result(i, 16, 32)
        send_result(i, 1, 16)
        res_in[i, mem] = res_out[i, mem]

    for i in range(2):
        take(res_in.at[i, some], res_r.at[i])
        for q in range(8):
            moved = dot(unpack, res_in[i, 4 * q:4 * q + 4].reshape(64, 768)).astype(BF)
            for k in range(4):
                out[k, i, 16 * q:16 * q + 16, :] = moved[16 * k:16 * k + 16]
        take(res_out.at[i, some], res_s.at[i])


def on_device(ensemble_state, obs_members, obs_values, obs_variance, obs_counts):
    vmem = pl.BlockSpec(memory_space=pltpu.VMEM)
    dma, dmas = pltpu.SemaphoreType.DMA(()), pltpu.SemaphoreType.DMA((2,))
    obs_box, state_box = pltpu.VMEM((32, 2, 16, 128), BF), pltpu.VMEM((32, 2, 16, 768), BF)
    res_box = pltpu.VMEM((2, 32, 16, 768), BF)
    sum_box = pltpu.VMEM((2, 4, ROWS, 128), F32)
    square = pltpu.VMEM((8, K, K), F32)
    return pl.pallas_call(
        kernel,
        out_shape=jax.ShapeDtypeStruct(ensemble_state.shape, BF),
        in_specs=[vmem, vmem, vmem, vmem, pl.BlockSpec(memory_space=pltpu.SMEM)],
        out_specs=vmem,
        scratch_shapes=[
            obs_box, obs_box, state_box, state_box, res_box, res_box,
            pltpu.VMEM((8, 2, EXT, 128), BF), pltpu.VMEM((8, 2, ROWS, 128), F32),
            sum_box, sum_box, sum_box, square, square, pltpu.VMEM((8, K, K), BF),
            pltpu.VMEM((512, 512), BF), pltpu.VMEM((512, 512), BF),
            dma, dma, dma, dma, dmas, dmas, dmas, dmas, dmas, dmas,
        ],
        compiler_params=pltpu.CompilerParams(
            collective_id=0, has_side_effects=True, vmem_limit_bytes=48 * 1024 * 1024
        ),
        cost_estimate=pl.CostEstimate(flops=10**10, bytes_accessed=4 * 10**6, transcendentals=0),
        name="letkf",
    )(ensemble_state, obs_members, obs_values, obs_variance, obs_counts)


def solution(mesh):
    placed = (
        P("mem", "tile", None, None),
        P("mem", "tile", None, None),
        P("tile", "mem", None),
        P("tile", "mem", None),
        P("tile", "mem"),
    )
    return jax.shard_map(
        on_device,
        mesh=mesh,
        in_specs=placed,
        out_specs=P("mem", "tile", None, None),
        check_vma=False,
    )
```

time: 307 us -> 218 us (0.71)
  the two profiles are of different devices: /device:TPU:32 before, /device:TPU:94 now
where the time goes in v1:
time: 218 us; the launch traced here: 217 us
  Pallas kernels  212 us (97%)
  local copies, waits for them, and re-layouts  5.55 us (3%)
    pallas_call x1, Pallas kernels, on_device(): pl.pallas_call(kernel, out_shape=jax.ShapeDtypeStruct(ensemble_state.shap...  212 us
    unnamed x11, local copies, waits for them, and re-layouts  5.55 us

profile of v1, /device:TPU:94, one launch (start us, length us, event | category | flops | bytes accessed | tf_op | source)
XLA Modules:
  0.0 217.3 jit_solution(1094226455322269237)
XLA Ops:
  0.0 0.0 copy-start
  0.0 1.4 copy-done
  1.4 0.0 copy-start.1
  1.4 0.9 copy-done.1
  2.4 0.0 copy-start.2
  2.4 0.7 copy-done.2
  3.0 0.0 copy-start.3
  3.0 0.7 copy-done.3
  3.7 0.0 copy-start.4
  3.7 0.7 copy-done.4
  4.4 211.8 %letkf.1 = bf16[4,2,128,768]{3,2,1,0:T(8,128)(2,1)S(1)} custom-call(bf16[4,2,128,768]{3,2,1,0:T(8,128)(2,1)S(1)} %copy-done, bf16[4,2,128,128]{3,2,1,0:T(8,128)(2,1)S(1)} %copy-done.1, f32[2,4,128]{2,1,0:T(4,128)S(1)} %copy-done.2, f32[2,4,128]{2,1,0:T(4,128)S(1)} %copy-done.3, s32[2,4]{1,0:T(2,128)S(1)} %copy-done.4), custom_call_target="tpu_custom_call" | custom-call | flops 10000000000 | bytes 4000000 | tf_op jit(solution)/shard_map/letkf/pallas_call | solution.py:334
  216.2 1.1 copy.7
Async XLA Ops:
  0.0 1.4 copy-start
  1.4 0.9 copy-start.1
  2.4 0.7 copy-start.2
  3.0 0.7 copy-start.3
  3.7 0.7 copy-start.4

commit v2 on v1

--- a/solution.py
+++ b/solution.py
@@ -18,6 +18,7 @@
 K = 128
 EXT = 144
 ROWS = 136
+FIRST = 2
 
 
 def iota(shape, dim):
@@ -71,13 +72,15 @@
 
 
 def kernel(
+    state_hbm, obs_hbm, values_hbm, variance_hbm, counts_hbm, out_hbm,
     state, obs, values, variance, counts, out,
     obs_out, obs_in, state_out, state_in, res_out, res_in,
-    scaled, grams, sums, above, below, root, inv, mix, perm, perm_back,
+    far_out, far_in, weights, far_weights, scaled, grams, sums, above, below, root, inv, mix, perm, perm_back,
+    load_s, store_s, far_s, far_r, weight_s, weight_r,
     obs_s, obs_r, state_s, state_r, col_s, col_r, row_s, row_r, res_s, res_r,
 ):
     mem, tile = lax.axis_index("mem"), lax.axis_index("tile")
-    mems, tiles = 32, 16
+    mems, tiles, middle = 32, 16, 15
     z, y, x = mem // 16, lax.rem(mem // 4, 4), lax.rem(mem, 4)
 
     def partner(step):
@@ -86,6 +89,13 @@
         px = lax.rem(x + lax.rem(step, 4), 4)
         return pz * 16 + py * 4 + px
 
+    loads = [
+        pltpu.make_async_copy(source, target, load_s.at[n]) for n, (source, target) in enumerate((
+            (obs_hbm, obs), (values_hbm, values), (variance_hbm, variance), (counts_hbm, counts),
+            (state_hbm, state)))
+    ]
+    for load in loads:
+        load.start()
     barrier = pltpu.get_barrier_semaphore()
 
     @pl.loop(1, mems)
@@ -104,16 +114,35 @@
     pack = one_hot(c == (r % 4) * 16 + (r // 16) * 4 + (r // 4) % 4)
     unpack = one_hot(r == (c % 4) * 16 + (c // 16) * 4 + (c // 4) % 4)
 
-    def packed(source, target):
+    def packed(source, target, far=None):
+        edges = ([], [])
         for i in range(2):
             for q in range(8):
                 rows = jnp.concatenate([source[k, i, 16 * q:16 * q + 16, :] for k in range(4)], axis=0)
-                moved = dot(pack, rows).astype(BF)
+                wide = dot(pack, rows)
+                moved = wide.astype(BF)
                 for d in range(4):
                     target[4 * q + d, i] = moved[16 * d:16 * d + 16]
-
-    packed(obs, obs_out)
+                if far is not None and q == 4:
+                    edges[0].append(wide[0:8])
+                if far is not None and q == 3:
+                    edges[1].append(wide[56:64])
+        if far is not None:
+            for side in range(2):
+                far[side] = jnp.concatenate(edges[side], axis=0).astype(BF)
+
+    loads[0].wait()
+    packed(obs, obs_out, far_out)
     obs_in[mem] = obs_out[mem]
+    for load in loads[1:4]:
+        load.wait()
+    slot = iota((1, 128), 1)
+    for i in range(2):
+        for j in range(4):
+            b = 4 * i + j
+            weights[0, b:b + 1] = jnp.where(
+                slot < counts[i, j], 1.0 / jnp.sqrt(variance[i, j:j + 1, :]), 0.0)
+            weights[1, b:b + 1] = values[i, j:j + 1, :]
 
     @pl.when(tile == 0)
     def _():
@@ -142,6 +171,27 @@
     send_all(obs_out, obs_in, obs_s, obs_r, 16, 32)
     send_all(obs_out, obs_in, obs_s, obs_r, 1, 16)
 
+    def to_middle(side):
+        return pltpu.make_async_remote_copy(
+            src_ref=far_out.at[side], dst_ref=far_in.at[mem], send_sem=far_s.at[side], recv_sem=far_r,
+            device_id={"mem": middle + side}, device_id_type=MESH)
+
+    def weights_over(side):
+        return pltpu.make_async_remote_copy(
+            src_ref=weights, dst_ref=far_weights, send_sem=weight_s, recv_sem=weight_r,
+            device_id={"mem": middle + 1 - side}, device_id_type=MESH)
+
+    for side in range(2):
+        @pl.when(mem != middle + side)
+        def _(side=side):
+            to_middle(side).start()
+
+        @pl.when(mem == middle + side)
+        def _(side=side):
+            weights_over(side).start()
+            far_in[mem] = far_out[side]
+
+    loads[4].wait()
     packed(state, state_out)
     state_in[mem] = state_out[mem]
     r, c = iota((512, 512), 0), iota((512, 512), 1)
@@ -150,21 +200,22 @@
 
     some = pl.ds(0, mems - 1)
     take(obs_out.at[some], obs_s)
-    send_all(state_out, state_in, state_s, state_r, 16, 32)
+    send_all(state_out, state_in, state_s, state_r, 16, 16 + FIRST)
     take(obs_in.at[some], obs_r)
 
-    slot = iota((1, 128), 1)
+    def scale(member, given, b, col, i):
+        mean = jnp.sum(member, axis=0, keepdims=True) * (1.0 / K)
+        weight = given[0, b:b + 1]
+        innovation = weight * (given[1, b:b + 1] - mean)
+        scaled[col, i, 0:K] = ((member - mean) * weight).astype(BF)
+        scaled[col, i, K:EXT] = jnp.where(
+            iota((16, 128), 0) == 0, jnp.broadcast_to(innovation, (16, 128)), 0.0
+        ).astype(BF)
+
     for i in range(2):
         wide = dot(perm[...], obs_in[:, i].reshape(512, 128))
         for j in range(4):
-            member = wide[128 * j:128 * j + 128]
-            mean = jnp.sum(member, axis=0, keepdims=True) * (1.0 / K)
-            weight = jnp.where(slot < counts[i, j], 1.0 / jnp.sqrt(variance[i, j:j + 1, :]), 0.0)
-            innovation = weight * (values[i, j:j + 1, :] - mean)
-            scaled[j + 2, i, 0:K] = ((member - mean) * weight).astype(BF)
-            scaled[j + 2, i, K:EXT] = jnp.where(
-                iota((16, 128), 0) == 0, jnp.broadcast_to(innovation, (16, 128)), 0.0
-            ).astype(BF)
+            scale(wide[128 * j:128 * j + 128], weights, 4 * i + j, j + 2, i)
 
     def to_left():
         return pltpu.make_async_remote_copy(
@@ -176,13 +227,31 @@
             src_ref=scaled.at[pl.ds(4, 2)], dst_ref=scaled.at[pl.ds(0, 2)], send_sem=col_s.at[1],
             recv_sem=col_r.at[1], device_id={"mem": mem + 1}, device_id_type=MESH)
 
-    @pl.when(mem > 0)
+    has_left = jnp.logical_and(mem != 0, mem != middle + 1)
+    has_right = jnp.logical_and(mem != mems - 1, mem != middle)
+
+    @pl.when(has_left)
     def _():
         to_left().start()
 
-    @pl.when(mem < mems - 1)
+    @pl.when(has_right)
     def _():
         to_right().start()
+
+    for side in range(2):
+        @pl.when(mem == middle + side)
+        def _(side=side):
+            take(far_in.at[some], far_r)
+            weights_over(side).wait()
+            wide = dot(perm[...], far_in[...].reshape(512, 128))
+            for i in range(2):
+                for jj in range(2):
+                    n = 2 * i + jj
+                    scale(wide[128 * n:128 * n + 128], far_weights, 4 * i + 2 * side + jj, 6 - 6 * side + jj, i)
+
+        @pl.when(mem != middle + side)
+        def _(side=side):
+            to_middle(side).wait_send()
 
     @pl.when(mem == 0)
     def _():
@@ -199,12 +268,12 @@
     for col in range(2, 6):
         gram(col)
 
-    @pl.when(mem > 0)
+    @pl.when(has_left)
     def _():
         to_left().wait_send()
         to_right().wait_recv()
 
-    @pl.when(mem < mems - 1)
+    @pl.when(has_right)
     def _():
         to_right().wait_send()
         to_left().wait_recv()
@@ -254,6 +323,7 @@
         to_below().wait_send()
         to_above().wait_recv()
 
+    send_all(state_out, state_in, state_s, state_r, 16 + FIRST, 32)
     send_all(state_out, state_in, state_s, state_r, 1, 16)
 
     eye = jnp.where(iota((K, K), 0) == iota((K, K), 1), 1.0, 0.0).astype(F32)
@@ -320,12 +390,17 @@
         for q in range(8):
             moved = dot(unpack, res_in[i, 4 * q:4 * q + 4].reshape(64, 768)).astype(BF)
             for k in range(4):
-                out[k, i, 16 * q:16 * q + 16, :] = moved[16 * k:16 * k + 16]
+                out[i, k, 16 * q:16 * q + 16, :] = moved[16 * k:16 * k + 16]
+        for k in range(4):
+            pltpu.make_async_copy(out.at[i, k], out_hbm.at[k, i], store_s.at[i, k]).start()
         take(res_out.at[i, some], res_s.at[i])
+    for i in range(2):
+        for k in range(4):
+            pltpu.make_async_copy(out.at[i, k], out_hbm.at[k, i], store_s.at[i, k]).wait()
 
 
 def on_device(ensemble_state, obs_members, obs_values, obs_variance, obs_counts):
-    vmem = pl.BlockSpec(memory_space=pltpu.VMEM)
+    hbm = pl.BlockSpec(memory_space=pl.ANY)
     dma, dmas = pltpu.SemaphoreType.DMA(()), pltpu.SemaphoreType.DMA((2,))
     obs_box, state_box = pltpu.VMEM((32, 2, 16, 128), BF), pltpu.VMEM((32, 2, 16, 768), BF)
     res_box = pltpu.VMEM((2, 32, 16, 768), BF)
@@ -334,17 +409,22 @@
     return pl.pallas_call(
         kernel,
         out_shape=jax.ShapeDtypeStruct(ensemble_state.shape, BF),
-        in_specs=[vmem, vmem, vmem, vmem, pl.BlockSpec(memory_space=pltpu.SMEM)],
-        out_specs=vmem,
+        in_specs=[hbm] * 5,
+        out_specs=hbm,
         scratch_shapes=[
+            pltpu.VMEM((4, 2, 128, 768), BF), pltpu.VMEM((4, 2, 128, 128), BF), pltpu.VMEM((2, 4, 128), F32),
+            pltpu.VMEM((2, 4, 128), F32), pltpu.SMEM((2, 4), jnp.int32), pltpu.VMEM((2, 4, 128, 768), BF),
             obs_box, obs_box, state_box, state_box, res_box, res_box,
+            pltpu.VMEM((2, 16, 128), BF), pltpu.VMEM((32, 16, 128), BF),
+            pltpu.VMEM((2, 8, 128), F32), pltpu.VMEM((2, 8, 128), F32),
             pltpu.VMEM((8, 2, EXT, 128), BF), pltpu.VMEM((8, 2, ROWS, 128), F32),
             sum_box, sum_box, sum_box, square, square, pltpu.VMEM((8, K, K), BF),
             pltpu.VMEM((512, 512), BF), pltpu.VMEM((512, 512), BF),
+            pltpu.SemaphoreType.DMA((5,)), pltpu.SemaphoreType.DMA((2, 4)), dmas, dma, dma, dma,
             dma, dma, dma, dma, dmas, dmas, dmas, dmas, dmas, dmas,
         ],
         compiler_params=pltpu.CompilerParams(
-            collective_id=0, has_side_effects=True, vmem_limit_bytes=48 * 1024 * 1024
+            collective_id=0, has_side_effects=True, vmem_limit_bytes=64 * 1024 * 1024
         ),
         cost_estimate=pl.CostEstimate(flops=10**10, bytes_accessed=4 * 10**6, transcendentals=0),
         name="letkf",

time: 218 us -> 201 us (0.922)
  the two profiles are of different devices: /device:TPU:94 before, /device:TPU:337 now
where the time goes in v2:
time: 201 us
  Pallas kernels  198 us (99%)
  local copies, waits for them, and re-layouts  2.65 us (1%)
    pallas_call x1, Pallas kernels, on_device(): pl.pallas_call(kernel, out_shape=jax.ShapeDtypeStruct(ensemble_state.shap...  198 us

profile of v2, /device:TPU:337, one launch (start us, length us, event | category | flops | bytes accessed | tf_op | source)
XLA Modules:
  0.0 200.6 jit_solution(15696516089751099912)
XLA Ops:
  0.0 197.9 %letkf.1 = bf16[4,2,128,768]{3,2,1,0:T(8,128)(2,1)} custom-call(bf16[4,2,128,768]{3,2,1,0:T(8,128)(2,1)} %state_hbm.1, bf16[4,2,128,128]{3,2,1,0:T(8,128)(2,1)} %obs_hbm.1, f32[2,4,128]{2,1,0:T(4,128)} %values_hbm.1, f32[2,4,128]{2,1,0:T(4,128)} %variance_hbm.1, s32[2,4]{1,0:T(2,128)} %counts_hbm.1), custom_call_target="tpu_custom_call" | custom-call | flops 10000000000 | bytes 4000000 | tf_op jit(solution)/shard_map/letkf/pallas_call | solution.py:409
  197.9 2.7 %copy.7 = bf16[4,2,128,768]{3,2,1,0:T(8,128)(2,1)} copy(bf16[4,2,128,768]{3,2,1,0:T(8,128)(2,1)} %letkf.1) | data formatting | bytes 3145728

commit v3 on v2

--- a/solution.py
+++ b/solution.py
@@ -18,7 +18,7 @@
 K = 128
 EXT = 144
 ROWS = 136
-FIRST = 2
+FIRST = 4
 
 
 def iota(shape, dim):
@@ -114,7 +114,7 @@
     pack = one_hot(c == (r % 4) * 16 + (r // 16) * 4 + (r // 4) % 4)
     unpack = one_hot(r == (c % 4) * 16 + (c // 16) * 4 + (c // 4) % 4)
 
-    def packed(source, target, far=None):
+    def packed(source, target, place, far=None):
         edges = ([], [])
         for i in range(2):
             for q in range(8):
@@ -122,7 +122,7 @@
                 wide = dot(pack, rows)
                 moved = wide.astype(BF)
                 for d in range(4):
-                    target[4 * q + d, i] = moved[16 * d:16 * d + 16]
+                    target[place(i, 4 * q + d)] = moved[16 * d:16 * d + 16]
                 if far is not None and q == 4:
                     edges[0].append(wide[0:8])
                 if far is not None and q == 3:
@@ -132,7 +132,7 @@
                 far[side] = jnp.concatenate(edges[side], axis=0).astype(BF)
 
     loads[0].wait()
-    packed(obs, obs_out, far_out)
+    packed(obs, obs_out, lambda i, to: (to, i), far_out)
     obs_in[mem] = obs_out[mem]
     for load in loads[1:4]:
         load.wait()
@@ -192,15 +192,15 @@
             far_in[mem] = far_out[side]
 
     loads[4].wait()
-    packed(state, state_out)
-    state_in[mem] = state_out[mem]
+    packed(state, state_out, lambda i, to: (i, to))
+    for i in range(2):
+        state_in[i, mem] = state_out[i, mem]
     r, c = iota((512, 512), 0), iota((512, 512), 1)
     perm[...] = one_hot(c == ((r // 4) % 32) * 16 + (r // 128) * 4 + r % 4)
     perm_back[...] = one_hot(r == ((c // 4) % 32) * 16 + (c // 128) * 4 + c % 4)
 
     some = pl.ds(0, mems - 1)
     take(obs_out.at[some], obs_s)
-    send_all(state_out, state_in, state_s, state_r, 16, 16 + FIRST)
     take(obs_in.at[some], obs_r)
 
     def scale(member, given, b, col, i):
@@ -265,6 +265,10 @@
         for i in range(2):
             grams[col, i] = dot_t(scaled[col, i], scaled[col, i, 0:K])[:ROWS]
 
+    def send_state(i, first, last):
+        send_all(state_out.at[i], state_in.at[i], state_s.at[i], state_r.at[i], first, last)
+
+    send_state(0, 16, 16 + FIRST)
     for col in range(2, 6):
         gram(col)
 
@@ -323,8 +327,10 @@
         to_below().wait_send()
         to_above().wait_recv()
 
-    send_all(state_out, state_in, state_s, state_r, 16 + FIRST, 32)
-    send_all(state_out, state_in, state_s, state_r, 1, 16)
+    send_state(0, 16 + FIRST, 32)
+    send_state(0, 1, 16)
+    send_state(1, 16, 32)
+    send_state(1, 1, 16)
 
     eye = jnp.where(iota((K, K), 0) == iota((K, K), 1), 1.0, 0.0).astype(F32)
     drives, norms = [], []
@@ -366,14 +372,12 @@
         shift = mul2(mul2(drives[b], right), right)[0:1]
         mix[b] = (math.sqrt(K - 1) * inverse + shift).astype(BF)
 
-    take(state_out.at[some], state_s)
-    take(state_in.at[some], state_r)
-
     def send_result(i, first, last):
         send_all(res_out.at[i], res_in.at[i], res_s.at[i], res_r.at[i], first, last)
 
     for i in range(2):
-        wide = dot(perm[...], state_in[:, i].reshape(512, 768))
+        take(state_in.at[i, some], state_r.at[i])
+        wide = dot(perm[...], state_in[i].reshape(512, 768))
         rows = []
         for j in range(4):
             member = wide[128 * j:128 * j + 128]
@@ -393,6 +397,7 @@
                 out[i, k, 16 * q:16 * q + 16, :] = moved[16 * k:16 * k + 16]
         for k in range(4):
             pltpu.make_async_copy(out.at[i, k], out_hbm.at[k, i], store_s.at[i, k]).start()
+        take(state_out.at[i, some], state_s.at[i])
         take(res_out.at[i, some], res_s.at[i])
     for i in range(2):
         for k in range(4):
@@ -402,8 +407,7 @@
 def on_device(ensemble_state, obs_members, obs_values, obs_variance, obs_counts):
     hbm = pl.BlockSpec(memory_space=pl.ANY)
     dma, dmas = pltpu.SemaphoreType.DMA(()), pltpu.SemaphoreType.DMA((2,))
-    obs_box, state_box = pltpu.VMEM((32, 2, 16, 128), BF), pltpu.VMEM((32, 2, 16, 768), BF)
-    res_box = pltpu.VMEM((2, 32, 16, 768), BF)
+    obs_box, row_box = pltpu.VMEM((32, 2, 16, 128), BF), pltpu.VMEM((2, 32, 16, 768), BF)
     sum_box = pltpu.VMEM((2, 4, ROWS, 128), F32)
     square = pltpu.VMEM((8, K, K), F32)
     return pl.pallas_call(
@@ -414,14 +418,14 @@
         scratch_shapes=[
             pltpu.VMEM((4, 2, 128, 768), BF), pltpu.VMEM((4, 2, 128, 128), BF), pltpu.VMEM((2, 4, 128), F32),
             pltpu.VMEM((2, 4, 128), F32), pltpu.SMEM((2, 4), jnp.int32), pltpu.VMEM((2, 4, 128, 768), BF),
-            obs_box, obs_box, state_box, state_box, res_box, res_box,
+            obs_box, obs_box, row_box, row_box, row_box, row_box,
             pltpu.VMEM((2, 16, 128), BF), pltpu.VMEM((32, 16, 128), BF),
             pltpu.VMEM((2, 8, 128), F32), pltpu.VMEM((2, 8, 128), F32),
             pltpu.VMEM((8, 2, EXT, 128), BF), pltpu.VMEM((8, 2, ROWS, 128), F32),
             sum_box, sum_box, sum_box, square, square, pltpu.VMEM((8, K, K), BF),
             pltpu.VMEM((512, 512), BF), pltpu.VMEM((512, 512), BF),
             pltpu.SemaphoreType.DMA((5,)), pltpu.SemaphoreType.DMA((2, 4)), dmas, dma, dma, dma,
-            dma, dma, dma, dma, dmas, dmas, dmas, dmas, dmas, dmas,
+            dma, dma, dmas, dmas, dmas, dmas, dmas, dmas, dmas, dmas,
         ],
         compiler_params=pltpu.CompilerParams(
             collective_id=0, has_side_effects=True, vmem_limit_bytes=64 * 1024 * 1024

time: 201 us -> 196 us (0.975)
  the two profiles are of different devices: /device:TPU:337 before, /device:TPU:161 now
where the time goes in v3:
time: 196 us; the launch traced here: 195 us
  Pallas kernels  193 us (98%)
  local copies, waits for them, and re-layouts  2.65 us (1%)
    pallas_call x1, Pallas kernels, on_device(): pl.pallas_call(kernel, out_shape=jax.ShapeDtypeStruct(ensemble_state.shap...  193 us

profile of v3, /device:TPU:161, one launch (start us, length us, event | category | flops | bytes accessed | tf_op | source)
XLA Modules:
  0.0 195.4 jit_solution(1286497525741898267)
XLA Ops:
  0.0 192.8 %letkf.1 = bf16[4,2,128,768]{3,2,1,0:T(8,128)(2,1)} custom-call(bf16[4,2,128,768]{3,2,1,0:T(8,128)(2,1)} %state_hbm.1, bf16[4,2,128,128]{3,2,1,0:T(8,128)(2,1)} %obs_hbm.1, f32[2,4,128]{2,1,0:T(4,128)} %values_hbm.1, f32[2,4,128]{2,1,0:T(4,128)} %variance_hbm.1, s32[2,4]{1,0:T(2,128)} %counts_hbm.1), custom_call_target="tpu_custom_call" | custom-call | flops 10000000000 | bytes 4000000 | tf_op jit(solution)/shard_map/letkf/pallas_call | solution.py:413
  192.8 2.7 %copy.7 = bf16[4,2,128,768]{3,2,1,0:T(8,128)(2,1)} copy(bf16[4,2,128,768]{3,2,1,0:T(8,128)(2,1)} %letkf.1) | data formatting | bytes 3145728

commit v4 on v3

--- a/solution.py
+++ b/solution.py
@@ -200,7 +200,11 @@
     perm_back[...] = one_hot(r == ((c // 4) % 32) * 16 + (c // 128) * 4 + c % 4)
 
     some = pl.ds(0, mems - 1)
+    def send_state(i, first, last):
+        send_all(state_out.at[i], state_in.at[i], state_s.at[i], state_r.at[i], first, last)
+
     take(obs_out.at[some], obs_s)
+    send_state(0, 1, 16)
     take(obs_in.at[some], obs_r)
 
     def scale(member, given, b, col, i):
@@ -265,9 +269,6 @@
         for i in range(2):
             grams[col, i] = dot_t(scaled[col, i], scaled[col, i, 0:K])[:ROWS]
 
-    def send_state(i, first, last):
-        send_all(state_out.at[i], state_in.at[i], state_s.at[i], state_r.at[i], first, last)
-
     send_state(0, 16, 16 + FIRST)
     for col in range(2, 6):
         gram(col)
@@ -328,7 +329,6 @@
         to_above().wait_recv()
 
     send_state(0, 16 + FIRST, 32)
-    send_state(0, 1, 16)
     send_state(1, 16, 32)
     send_state(1, 1, 16)
 

time: 196 us -> 196 us (level)
  the two profiles are of different devices: /device:TPU:161 before, /device:TPU:128 now
where the time goes in v4:
time: 196 us
  Pallas kernels  193 us (98%)
  local copies, waits for them, and re-layouts  2.65 us (1%)
    pallas_call x1, Pallas kernels, on_device(): pl.pallas_call(kernel, out_shape=jax.ShapeDtypeStruct(ensemble_state.shap...  193 us

profile of v4, /device:TPU:128, one launch (start us, length us, event | category | flops | bytes accessed | tf_op | source)
XLA Modules:
  0.0 195.8 jit_solution(1255508513512663937)
XLA Ops:
  0.0 193.1 %letkf.1 = bf16[4,2,128,768]{3,2,1,0:T(8,128)(2,1)} custom-call(bf16[4,2,128,768]{3,2,1,0:T(8,128)(2,1)} %state_hbm.1, bf16[4,2,128,128]{3,2,1,0:T(8,128)(2,1)} %obs_hbm.1, f32[2,4,128]{2,1,0:T(4,128)} %values_hbm.1, f32[2,4,128]{2,1,0:T(4,128)} %variance_hbm.1, s32[2,4]{1,0:T(2,128)} %counts_hbm.1), custom_call_target="tpu_custom_call" | custom-call | flops 10000000000 | bytes 4000000 | tf_op jit(solution)/shard_map/letkf/pallas_call | solution.py:413
  193.1 2.7 %copy.7 = bf16[4,2,128,768]{3,2,1,0:T(8,128)(2,1)} copy(bf16[4,2,128,768]{3,2,1,0:T(8,128)(2,1)} %letkf.1) | data formatting | bytes 3145728
